TPU v7x, 32 devices: a whole 2x2x4 slice. The times are simulated.
32 devices in a mesh: groups: 2 (over y), lat: 4 (over z), lon: 2 (over x), section: 2 (over core).
Axes of the slice: x: 2, y: 2, z: 4, core: 2. Of those that a mesh axis runs over, the one named last changes fastest.
Arguments:
- features: bfloat16 [4, 200, 32, 256], P('groups', None, 'lat', 'lon'), parts along dimension 0, may hold values from -6 to 6
- ocean_tiles: int32 [4, 32], P('lat', 'lon'), may hold values 0 or 1
- kernels: float32 [2, 200, 49], P('section'), may hold values from -0.875 to 0.875
- norm_gains: float32 [2, 200], P('section'), may hold values from 0.5 to 2
- weights_in: bfloat16 [2, 200, 800], P('section'), may hold values from -0.4375 to 0.4375
- biases_in: float32 [2, 800], P('section'), may hold values from -3 to 3
- weights_out: bfloat16 [2, 800, 200], P('section'), may hold values from -0.21875 to 0.21875
Outputs:
- section_features: bfloat16 [2, 4, 200, 32, 256], P('section', 'groups', None, 'lat', 'lon'), parts along dimension 1
There are 2 independent parts, one for each index of `groups`. A program takes and returns all parts, laid end to end along the dimension named above; an argument that names none is the same for every part. Nothing has to cross between parts.
Inputs may be any that keep to these rules, and one draw needn't show every extreme that they name: `ocean_tiles`: 1 marks a tile of 8 x 8 cells as ocean, 0 as land.
All inputs are finite; a program needn't handle non-finite values. No bound on the sum of `ocean_tiles` on one device may be relied on, other than what follows from the above.
Results may differ from a plain program's by a relative error of at most 0.018.
Values may be sent and summed in bfloat16 or wider, within the bound.
A program may use at most 64 MiB of HBM per device.

v0:
```python
import functools

import jax
import jax.numpy as jnp
from jax import lax
from jax.experimental import pallas as pl
from jax.experimental.pallas import tpu as pltpu
from jax.sharding import PartitionSpec as P

MESH = pl.DeviceIdType.MESH
KSIZE = 7
REACH = 3
TILE = 8
BLOCK = 16
BF = jnp.bfloat16
F32 = jnp.float32


def selection(shape, fn):
    r = lax.broadcasted_iota(jnp.int32, shape, 0)
    c = lax.broadcasted_iota(jnp.int32, shape, 1)
    return jnp.where(fn(r, c), 1.0, 0.0).astype(BF)


def dot(a, b):
    return jnp.dot(a, b, preferred_element_type=F32)


def kernel(n_lat, n_lon, ch, hid, rows, cols, chp,
           x_ref, tiles_ref, ker_ref, gain_ref, wi_ref, bias_ref, wo_ref, out_ref,
           ker_s, gain_s, wi_s, bias_s, wo_s, xp, hal, nb, pk, pw, pe, pc, pcn, pcs, zz,
           smat, umat, utn, kb, gb, wit, wot, mixed, nrm, act,
           loc_sem, wsend, wrecv, psend, precv, rsend, rrecv, csend, crecv, osend, orecv):
    lat = lax.axis_index("lat")
    lon = lax.axis_index("lon")
    sec = lax.axis_index("section")
    is_top = lat == n_lat - 1
    has_south = lat > 0
    partner = {"section": 1 - sec}
    north = {"lat": jnp.where(is_top, lat, lat + 1), "lon": jnp.where(is_top, n_lon - 1 - lon, lon)}
    south = {"lat": jnp.where(has_south, lat - 1, lat)}
    east = lax.rem(lon + 1, n_lon)
    west = lax.rem(lon + n_lon - 1, n_lon)
    sides = [({"lon": west}, pe)] if n_lon == 2 else [({"lon": west}, pe), ({"lon": east}, pw)]
    pairs = rows // 2
    tiles = chp // BLOCK

    load = pltpu.make_async_copy(x_ref, xp.at[0, pl.ds(REACH, rows)], loc_sem.at[5])
    load.start()
    barrier = pltpu.get_barrier_semaphore()
    pl.semaphore_signal(barrier, inc=1, device_id=partner, device_id_type=MESH)
    pl.semaphore_signal(barrier, inc=1, device_id=north, device_id_type=MESH)
    for device, _ in sides:
        pl.semaphore_signal(barrier, inc=1, device_id=device, device_id_type=MESH)

    @pl.when(has_south)
    def _():
        pl.semaphore_signal(barrier, inc=1, device_id=south, device_id_type=MESH)

    @pl.when(lat == 0)
    def _():
        for s in range(2):
            xp[s, 0:REACH] = jnp.zeros((REACH, chp, cols), BF)
            pcs[s] = jnp.zeros((2, 2 * BLOCK, cols), BF)

    smat[...] = selection((2 * cols, cols), lambda r, c: (
        ((r % cols < REACH) & (c % 16 == (r // cols) * 8 + r % cols))
        | ((r % cols >= cols - REACH) & (c % 16 == (r // cols) * 8 + 4 + r % cols - (cols - REACH)))))
    flip = selection((cols, cols), lambda r, c: r == cols - 1 - c).astype(F32)
    ident = selection((cols, cols), lambda r, c: r == c).astype(F32)
    turn = jnp.where(is_top, flip, ident).astype(BF)
    for q in range(2):
        unit = selection((cols, cols), lambda r, c: (
            ((c < REACH) & (r == 8 * q + c)) | ((c >= cols - REACH) & (r == 8 * q + 4 + c - (cols - REACH)))))
        umat[q] = unit
        utn[q] = dot(unit, turn).astype(BF)

    def pack(s, i):
        both = jnp.concatenate([xp[s, REACH + 2 * i], xp[s, REACH + 2 * i + 1]], axis=1)
        spread = dot(both, smat[...])
        group = lax.broadcasted_iota(jnp.int32, (BLOCK, cols), 1) // 16
        for h in range(2):
            total = jnp.zeros((BLOCK, cols), F32)
            for t in range(8 * h, min(8 * h + 8, tiles)):
                total = jnp.where(group == t % 8, spread[t * BLOCK:(t + 1) * BLOCK], total)
            pk[s, i, h * BLOCK:(h + 1) * BLOCK] = total.astype(BF)

    def pack_copies(s, i):
        return [pltpu.make_async_remote_copy(
            src_ref=pk.at[s, i], dst_ref=dst.at[s, i], send_sem=psend.at[s, i, k], recv_sem=precv.at[s, i, k],
            device_id=device, device_id_type=MESH) for k, (device, dst) in enumerate(sides)]

    def remote(src, dst, send, recv, device):
        return pltpu.make_async_remote_copy(
            src_ref=src, dst_ref=dst, send_sem=send, recv_sem=recv, device_id=device, device_id_type=MESH)

    def rows_north(s, part):
        at, into, fold, size = ((rows + 1, 1, 1, 2), (rows, 0, 0, 1))[part]
        block = xp.at[s, pl.ds(at, size)]
        send = rsend.at[s, 0, part]
        return (remote(block, xp.at[s, pl.ds(into, size)], send, rrecv.at[s, 0, part], north),
                remote(block, nb.at[s, pl.ds(fold, size)], send, rrecv.at[s, 1, part], north))

    def rows_south(s, part):
        at, into, size = ((REACH, 0, 2), (REACH + 2, 2, 1))[part]
        return remote(xp.at[s, pl.ds(at, size)], nb.at[s, pl.ds(into, size)],
                      rsend.at[s, 1, part], rrecv.at[s, 1, part], south)

    def packs_north(s):
        block = pc.at[s, pl.ds(pairs - 2, 2)]
        return (remote(block, pcs.at[s], csend.at[s, 0], crecv.at[s, 0], north),
                remote(block, pcn.at[s], csend.at[s, 0], crecv.at[s, 1], north))

    def packs_south(s):
        return remote(pc.at[s, pl.ds(0, 2)], pcn.at[s], csend.at[s, 1], crecv.at[s, 1], south)

    def start_north(copies):
        @pl.when(is_top)
        def _():
            copies[1].start()

        @pl.when(jnp.logical_not(is_top))
        def _():
            copies[0].start()

    def if_south(act_on):
        @pl.when(has_south)
        def _():
            act_on()

    def combine(s, i):
        for copy in pack_copies(s, i):
            copy.wait_recv()
        if n_lon == 2:
            pc[s, i] = pe[s, i]
        else:
            lane = lax.broadcasted_iota(jnp.int32, (2 * BLOCK, cols), 1)
            pc[s, i] = jnp.where(lane % 8 < 4, pe[s, i].astype(F32), pw[s, i].astype(F32)).astype(BF)

    def unpack(packed):
        for t in range(tiles):
            part = packed[(t // 8) * BLOCK:(t // 8 + 1) * BLOCK]
            zz[t * BLOCK:(t + 1) * BLOCK] = pltpu.roll(part, (-16 * (t % 8)) % cols, 1) if t % 8 else part
        return zz[...]

    def prepare_conv(s):
        gain = gain_s[s]
        diag = lax.broadcasted_iota(jnp.int32, (ch, ch), 0) == lax.broadcasted_iota(jnp.int32, (ch, ch), 1)
        column = jnp.sum(jnp.where(diag, jnp.broadcast_to(gain, (ch, ch)), 0.0), axis=1, keepdims=True)
        gb[s] = jnp.broadcast_to(column, (ch, cols))
        taps = ker_s[s].T
        for t in range(KSIZE * KSIZE):
            kb[s, t, 0:ch] = jnp.broadcast_to(taps[:, t:t + 1], (ch, cols))
            kb[s, t, ch:chp] = jnp.zeros((chp - ch, cols), F32)

    def prepare_weights(s):
        b = bias_s[s]
        hi = b.astype(BF).astype(F32)
        mid = (b - hi).astype(BF).astype(F32)
        low = (b - hi - mid).astype(BF).astype(F32)
        tail = jnp.concatenate([hi, mid, low, jnp.zeros((chp - ch - 3, hid), F32)], axis=0)
        whole = jnp.concatenate([wi_s[s].astype(F32), tail], axis=0)
        wit[s] = whole.T.astype(BF)
        wot[s] = (wo_s[s].astype(F32) * 0.5).astype(BF)

    tail_row = lax.broadcasted_iota(jnp.int32, (chp - ch, cols), 0)
    ones_tail = jnp.where(tail_row < 3, 1.0, 0.0).astype(F32)
    tile_cols = tiles_ref.shape[1]
    spread_tiles = selection((tile_cols, cols), lambda r, c: c // TILE == r)
    mask = dot(jnp.broadcast_to(tiles_ref[...].astype(F32).astype(BF), (8, tile_cols)), spread_tiles)[0:1]
    mask2 = jnp.concatenate([mask, mask], axis=1)

    load.wait()
    for i in range(pairs):
        pack(0, i)
    pl.semaphore_wait(barrier, 2 + len(sides) + jnp.where(has_south, 1, 0))

    params = [(ker_ref, ker_s), (gain_ref, gain_s), (bias_ref, bias_s), (wi_ref, wi_s), (wo_ref, wo_s)]
    moved = []
    for i in range(pairs):
        for copy in pack_copies(0, i):
            copy.start()
    for k, (src, dst) in enumerate(params):
        copy = remote(src, dst.at[sec], wsend.at[k], wrecv.at[k], partner)
        copy.start()
        own = pltpu.make_async_copy(src, dst.at[sec], loc_sem.at[k])
        own.start()
        moved.append((copy, own))
        if k == 1:
            for part in range(2):
                start_north(rows_north(0, part))
                if_south(rows_south(0, part).start)

    def wait_params(k):
        moved[k][1].wait()
        moved[k][0].wait()

    def shift(x, h, d, lane):
        if d == 0:
            return x.astype(F32)
        x = jnp.where(lane < d if d > 0 else lane >= cols + d, h, x)
        return pltpu.roll(x, (-d) % cols, 1).astype(F32)

    def conv_pass(s, sources, first):
        def body(t, carry):
            at = pl.ds(pl.multiple_of(t * BLOCK, BLOCK), BLOCK)
            lane = lax.broadcasted_iota(jnp.int32, (BLOCK, cols), 1)
            acc = {}
            for b in range(KSIZE):
                d = b - REACH
                shifted = {r: shift(xp[s, r, at, :], hal[r, at, :] if d else None, d, lane) for r in sources}
                for a in range(KSIZE):
                    used = [j for j in range(rows) if j + a in shifted]
                    if not used:
                        continue
                    weight = kb[s, a * KSIZE + b, at, :]
                    for j in used:
                        term = weight * shifted[j + a]
                        acc[j] = acc[j] + term if j in acc else term
            for j in acc:
                mixed[j, at, :] = acc[j] if first else mixed[j, at, :] + acc[j]
            return carry

        lax.fori_loop(0, tiles, body, 0)

    def out_copies(s, i):
        block = xp.at[s + 1, pl.ds(REACH + 2 * i, 2)]
        into = out_ref.at[sec, pl.ds(2 * i, 2)]
        return (pltpu.make_async_copy(block, into, osend.at[s, i]),
                remote(block, into, osend.at[s, i], orecv.at[i], partner))

    def point(s, i):
        for k in range(2):
            m = mixed[2 * i + k, 0:ch, :]
            centre = jnp.sum(m, axis=0, keepdims=True) * (1.0 / ch)
            m = m - centre
            var = jnp.sum(m * m, axis=0, keepdims=True) * (1.0 / ch)
            m = m * lax.rsqrt(var + 1e-6) * gb[s]
            nrm[:, k * cols:(k + 1) * cols] = jnp.concatenate([m, ones_tail], axis=0).astype(BF)
        chunk = 160
        for q in range(hid // chunk):
            h = dot(wit[s, q * chunk:(q + 1) * chunk], nrm[...])
            act[q * chunk:(q + 1) * chunk] = (h * (1.0 + lax.erf(h * 0.7071067811865476))).astype(BF)
        update = dot(wot[s], act[...]) * mask2
        for k in range(2):
            row = REACH + 2 * i + k
            x = xp[s, row, 0:ch, :].astype(F32) + update[:, k * cols:(k + 1) * cols]
            xp[s + 1, row] = jnp.concatenate([x, jnp.zeros((chp - ch, cols), F32)], axis=0).astype(BF)
        here, there = out_copies(s, i)

        @pl.when(sec == s)
        def _():
            here.start()

        @pl.when(sec != s)
        def _():
            there.start()

    for s in range(2):
        if s == 0:
            wait_params(0)
            wait_params(1)
            prepare_conv(0)
        for i in range(pairs - 1, pairs - 3, -1):
            combine(s, i)
        start_north(packs_north(s))
        if s == 1:
            prepare_conv(1)
        for i in range(2):
            combine(s, i)
        if_south(packs_south(s).start)
        for i in range(pairs):
            held = unpack(pc[s, i])
            for q in range(2):
                hal[REACH + 2 * i + q] = dot(held, umat[q]).astype(BF)
        conv_pass(s, range(REACH, REACH + rows), True)
        if s == 0:
            for k in range(2, 5):
                wait_params(k)
            prepare_weights(0)
            prepare_weights(1)
        for part in range(2):
            rows_north(s, part)[1].wait_recv()
            if_south(rows_north(s, part)[0].wait_recv)
        packs_north(s)[1].wait_recv()
        if_south(packs_north(s)[0].wait_recv)
        for k in range(REACH):
            row = jnp.where(is_top, REACH - 1 - k, k)
            xp[s, REACH + rows + k] = dot(nb[s, row], turn).astype(BF)
        for p in range(2):
            held = unpack(pcn[s, jnp.where(is_top, 1 - p, p)])
            for q in range(2):
                k = 2 * p + q
                if k < REACH:
                    hal[REACH + rows + k] = dot(held, utn[jnp.where(is_top, 1 - q, q)]).astype(BF)
            held = unpack(pcs[s, p])
            for q in range(2):
                k = 2 * p + q - 1
                if k >= 0:
                    hal[k] = dot(held, umat[q]).astype(BF)
        conv_pass(s, [*range(REACH), *range(REACH + rows, 2 * REACH + rows)], False)
        for i in (pairs - 1, 0, pairs - 2, 1):
            point(s, i)
            if s == 0:
                part = 0 if i in (0, pairs - 1) else 1
                if i >= pairs - 2:
                    start_north(rows_north(1, part))
                else:
                    if_south(rows_south(1, part).start)
                pack(1, i)
                for copy in pack_copies(1, i):
                    copy.start()

    for s in range(2):
        for i in range(pairs):
            here, there = out_copies(s, i)

            @pl.when(sec == s)
            def _():
                here.wait()

            @pl.when(sec != s)
            def _():
                there.wait_send()

            for copy in pack_copies(s, i):
                copy.wait_send()
        for part in range(2):
            rows_north(s, part)[0].wait_send()
            if_south(rows_south(s, part).wait_send)
        packs_north(s)[0].wait_send()
        if_south(packs_south(s).wait_send)
    for i in range(pairs):
        out_copies(0, i)[1].wait_recv()


def on_device(features, ocean_tiles, kernels, norm_gains, weights_in, biases_in, weights_out):
    n_lat, n_lon = lax.axis_size("lat"), lax.axis_size("lon")
    micro, ch, rows, cols = features.shape
    hid = weights_in.shape[2]
    chp = -(-ch // BLOCK) * BLOCK
    padded = rows + 2 * REACH
    state = lax.dynamic_index_in_dim(features, lax.axis_index("section"), 0, keepdims=False)
    state = jnp.pad(state.transpose(1, 0, 2), ((0, 0), (0, chp - ch), (0, 0)))
    any_spec = pl.BlockSpec(memory_space=pl.ANY)
    vmem = pl.BlockSpec(memory_space=pltpu.VMEM)
    V = pltpu.VMEM
    dma = pltpu.SemaphoreType.DMA
    pairs = rows // 2
    pack = (2, pairs, 2 * BLOCK, cols)
    edge = (2, 2, 2 * BLOCK, cols)
    hbm = pl.BlockSpec(memory_space=pltpu.HBM)
    out = pl.pallas_call(
        functools.partial(kernel, n_lat, n_lon, ch, hid, rows, cols, chp),
        out_shape=jax.ShapeDtypeStruct((micro, rows, chp, cols), BF),
        in_specs=[any_spec, vmem] + [hbm] * 5,
        out_specs=any_spec,
        scratch_shapes=[
            V((2, KSIZE * KSIZE, ch), F32), V((2, 1, ch), F32), V((2, ch, hid), BF), V((2, 1, hid), F32),
            V((2, ch, hid), BF),
            V((3, padded, chp, cols), BF), V((padded, chp, cols), BF), V((2, REACH, chp, cols), BF),
            V(pack, BF), V(pack, BF), V(pack, BF), V(pack, BF), V(edge, BF), V(edge, BF), V((chp, cols), BF),
            V((2 * cols, cols), BF), V((2, cols, cols), BF), V((2, cols, cols), BF),
            V((2, KSIZE * KSIZE, chp, cols), F32), V((2, ch, cols), F32), V((2, hid, chp), BF), V((2, ch, hid), BF),
            V((rows, chp, cols), F32), V((chp, 2 * cols), BF), V((hid, 2 * cols), BF),
            dma((6,)), dma((5,)), dma((5,)), dma((2, pairs, 2)), dma((2, pairs, 2)), dma((2, 2, 2)), dma((2, 2, 2)),
            dma((2, 2)), dma((2, 2)), dma((2, pairs)), dma((pairs,)),
        ],
        compiler_params=pltpu.CompilerParams(
            collective_id=0, has_side_effects=True, vmem_limit_bytes=40 * 1024 * 1024),
    )(state, ocean_tiles, kernels[0].T, norm_gains, weights_in[0], biases_in, weights_out[0].T)
    return out[:, :, :ch, :].transpose(0, 2, 1, 3)[None]


def solution(mesh):
    return jax.shard_map(
        on_device,
        mesh=mesh,
        in_specs=(
            P("groups", None, "lat", "lon"),
            P("lat", "lon"),
            P("section", None, None),
            P("section", None),
            P("section", None, None),
            P("section", None),
            P("section", None, None),
        ),
        out_specs=P("section", "groups", None, "lat", "lon"),
        check_vma=False,
    )
```

profile of v0, /device:TPU:0, one launch (start us, length us, event | category | flops | bytes accessed | tf_op | source)
XLA Modules:
  0.0 33.5 jit_solution(2734597895115256785)
XLA Ops:
  0.0 0.0 copy-start
  0.0 0.9 %copy.14 = f32[1,200,49]{1,2,0:T(8,128)S(1)} copy(f32[1,200,49]{1,0,2:T(1,128)} %param.9) | data formatting | bytes 78400
  0.9 0.3 copy-done
  1.2 0.1 copy.13
  1.3 0.0 copy-start.1
  1.3 0.0 copy-start.2
  1.3 0.0 copy-start.3
  1.3 0.0 copy-start.4
  1.3 0.0 copy-start.5
  1.4 0.9 %copy-done.1 = bf16[1,200,800]{2,1,0:T(8,128)(2,1)S(1)} copy-done((bf16[1,200,800]{2,1,0:T(8,128)(2,1)S(1)}, bf16[1,200,800]{2,1,0:T(8,128)(2,1)}, u32[]{:S(2)}) %copy-start.1) | copy-done | bytes 320024
  2.3 0.1 copy-done.2
  2.4 0.0 copy-done.3
  2.4 0.0 copy-done.4
  2.4 0.0 copy-done.5
  2.4 30.1 %shard_map.73 = bf16[2,8,208,128]{3,2,1,0:T(8,128)(2,1)S(1)} custom-call(bf16[8,208,128]{2,1,0:T(8,128)(2,1)S(1)} %pad.4.x_ref, s32[1,16]{1,0:T(1,128)S(1)} %copy-done.5, f32[49,200]{1,0:T(8,128)S(1)} %bitcast.20, f32[1,200]{1,0:T(1,128)S(1)} %copy-done.4, bf16[200,800]{1,0:T(8,128)(2,1)S(1)} %bitcast.18, f32[1,800]{1,0:T(1,128)S(1)} %copy-done.3, ...), custom_call_target="tpu_custom_call" | custom-call | tf_op jit(solution)/shard_map/pallas_call | solution.py:353
  32.5 0.1 slice_bitcast_fusion
  32.5 1.0 %copy.9 = bf16[1,2,200,8,128]{4,3,2,1,0:T(8,128)(2,1)} copy(bf16[1,2,200,8,128]{4,2,3,1,0:T(8,128)(2,1)S(1)} %slice_bitcast_fusion) | data formatting | bytes 1638400 | tf_op jit(solution)/shard_map/broadcast_in_dim | solution.py:372
  (2 shorter events, 0.1 us)
Async XLA Ops:
  0.0 1.2 %copy-start = (bf16[2,200,8,128]{3,2,1,0:T(8,128)(2,1)S(1)}, bf16[2,200,8,128]{3,2,1,0:T(8,128)(2,1)}, u32[]{:S(2)}) copy-start(bf16[2,200,8,128]{3,2,1,0:T(8,128)(2,1)} %param.7) | copy-start | bytes 2457604
  1.3 1.0 %copy-start.1 = (bf16[1,200,800]{2,1,0:T(8,128)(2,1)S(1)}, bf16[1,200,800]{2,1,0:T(8,128)(2,1)}, u32[]{:S(2)}) copy-start(bf16[1,200,800]{2,1,0:T(8,128)(2,1)} %param.11) | copy-start | bytes 960004
  1.3 1.1 %copy-start.2 = (bf16[1,800,200]{1,2,0:T(8,128)(2,1)S(1)}, bf16[1,800,200]{1,2,0:T(8,128)(2,1)}, u32[]{:S(2)}) copy-start(bf16[1,800,200]{1,2,0:T(8,128)(2,1)} %param.13) | copy-start | bytes 960004
  1.3 1.1 %copy-start.3 = (f32[1,800]{1,0:T(1,128)S(1)}, f32[1,800]{1,0:T(1,128)}, u32[]{:S(2)}) copy-start(f32[1,800]{1,0:T(1,128)} %bias_ref.1) | copy-start | bytes 9604
  1.3 1.1 %copy-start.4 = (f32[1,200]{1,0:T(1,128)S(1)}, f32[1,200]{1,0:T(1,128)}, u32[]{:S(2)}) copy-start(f32[1,200]{1,0:T(1,128)} %gain_ref.1) | copy-start | bytes 2404
  1.3 1.1 %copy-start.5 = (s32[1,16]{1,0:T(1,128)S(1)}, s32[1,16]{1,0:T(1,128)}, u32[]{:S(2)}) copy-start(s32[1,16]{1,0:T(1,128)} %tiles_ref.1) | copy-start | bytes 196
where the time goes:
time: 33.7 us; the launch traced here: 33.5 us
  Pallas kernels  30.1 us (89%)
  local copies, waits for them, and re-layouts  3.36 us (10%)
    pallas_call x1, Pallas kernels, on_device(): pl.pallas_call(functools.partial(kernel, n_lat, n_lon, ch, hid, rows, col...  30.1 us
    unnamed x13, local copies, waits for them, and re-layouts  2.19 us
    broadcast_in_dim x2, local copies, waits for them, and re-layouts, on_device(): return out[:, :, :ch, :].transpose(0, 2, 1, 3)[None]  1.06 us

commit v1 on v0

--- a/solution.py
+++ b/solution.py
@@ -148,7 +148,7 @@
         diag = lax.broadcasted_iota(jnp.int32, (ch, ch), 0) == lax.broadcasted_iota(jnp.int32, (ch, ch), 1)
         column = jnp.sum(jnp.where(diag, jnp.broadcast_to(gain, (ch, ch)), 0.0), axis=1, keepdims=True)
         gb[s] = jnp.broadcast_to(column, (ch, cols))
-        taps = ker_s[s].T
+        taps = ker_s[s, :, 0, :].T
         for t in range(KSIZE * KSIZE):
             kb[s, t, 0:ch] = jnp.broadcast_to(taps[:, t:t + 1], (ch, cols))
             kb[s, t, ch:chp] = jnp.zeros((chp - ch, cols), F32)
@@ -221,7 +221,7 @@
                 mixed[j, at, :] = acc[j] if first else mixed[j, at, :] + acc[j]
             return carry
 
-        lax.fori_loop(0, tiles, body, 0)
+        lax.fori_loop(0, tiles, body, 0, unroll=not first)
 
     def out_copies(s, i):
         block = xp.at[s + 1, pl.ds(REACH + 2 * i, 2)]
@@ -356,7 +356,7 @@
         in_specs=[any_spec, vmem] + [hbm] * 5,
         out_specs=any_spec,
         scratch_shapes=[
-            V((2, KSIZE * KSIZE, ch), F32), V((2, 1, ch), F32), V((2, ch, hid), BF), V((2, 1, hid), F32),
+            V((2, KSIZE * KSIZE, 1, ch), F32), V((2, 1, ch), F32), V((2, ch, hid), BF), V((2, 1, hid), F32),
             V((2, ch, hid), BF),
             V((3, padded, chp, cols), BF), V((padded, chp, cols), BF), V((2, REACH, chp, cols), BF),
             V(pack, BF), V(pack, BF), V(pack, BF), V(pack, BF), V(edge, BF), V(edge, BF), V((chp, cols), BF),
@@ -368,7 +368,7 @@
         ],
         compiler_params=pltpu.CompilerParams(
             collective_id=0, has_side_effects=True, vmem_limit_bytes=40 * 1024 * 1024),
-    )(state, ocean_tiles, kernels[0].T, norm_gains, weights_in[0], biases_in, weights_out[0].T)
+    )(state, ocean_tiles, kernels.transpose(2, 0, 1), norm_gains, weights_in[0], biases_in, weights_out[0].T)
     return out[:, :, :ch, :].transpose(0, 2, 1, 3)[None]
 
 

time: 33.7 us -> 31.8 us (0.944)
  Pallas kernels: 30.1 us -> 28.2 us
    pallas_call x1, Pallas kernels: 30.1 us -> 28.2 us  [on_device(): pl.pallas_call(functools.partial(kernel, n_lat, n_lon, ch, hid, rows, col...]
    unnamed x13 -> x14, local copies, waits for them, and re-layouts: 2.19 us -> 2.16 us
where the time goes in v1:
time: 31.8 us; the launch traced here: 31.7 us
  Pallas kernels  28.2 us (89%)
  local copies, waits for them, and re-layouts  3.33 us (10%)
    pallas_call x1, Pallas kernels, on_device(): pl.pallas_call(functools.partial(kernel, n_lat, n_lon, ch, hid, rows, col...  28.2 us
    unnamed x14, local copies, waits for them, and re-layouts  2.16 us
    broadcast_in_dim x2, local copies, waits for them, and re-layouts, on_device(): return out[:, :, :ch, :].transpose(0, 2, 1, 3)[None]  1.06 us

profile of v1, /device:TPU:0, one launch (start us, length us, event | category | flops | bytes accessed | tf_op | source)
XLA Modules:
  0.0 31.7 jit_solution(15556808344694472474)
XLA Ops:
  0.0 0.0 copy-start
  0.0 1.1 %copy-done = bf16[2,200,8,128]{3,2,1,0:T(8,128)(2,1)S(1)} copy-done((bf16[2,200,8,128]{3,2,1,0:T(8,128)(2,1)S(1)}, bf16[2,200,8,128]{3,2,1,0:T(8,128)(2,1)}, u32[]{:S(2)}) %copy-start) | copy-done | bytes 819224
  1.2 0.1 copy.11
  1.2 0.0 copy-start.1
  1.3 0.0 copy-start.2
  1.3 0.0 copy-start.3
  1.3 0.0 copy-start.4
  1.3 0.0 copy-start.5
  1.3 0.0 copy-start.6
  1.4 0.9 %copy-done.1 = bf16[1,200,800]{2,1,0:T(8,128)(2,1)S(1)} copy-done((bf16[1,200,800]{2,1,0:T(8,128)(2,1)S(1)}, bf16[1,200,800]{2,1,0:T(8,128)(2,1)}, u32[]{:S(2)}) %copy-start.1) | copy-done | bytes 320024
  2.2 0.1 copy-done.2
  2.3 0.0 copy-done.3
  2.3 0.0 copy-done.4
  2.3 0.0 copy-done.5
  2.3 0.0 copy-done.6
  2.4 28.2 %shard_map.73 = bf16[2,8,208,128]{3,2,1,0:T(8,128)(2,1)S(1)} custom-call(bf16[8,208,128]{2,1,0:T(8,128)(2,1)S(1)} %pad.4.x_ref, s32[1,16]{1,0:T(1,128)S(1)} %copy-done.6, f32[49,1,200]{2,1,0:T(1,128)S(1)} %bitcast.16, f32[1,200]{1,0:T(1,128)S(1)} %copy-done.5, bf16[200,800]{1,0:T(8,128)(2,1)S(1)} %bitcast.14, f32[1,800]{1,0:T(1,128)S(1)} %copy-done.4, ...), custom_call_target="tpu_custom_call" | custom-call | tf_op jit(solution)/shard_map/pallas_call | solution.py:353
  30.6 0.1 slice_bitcast_fusion
  30.7 1.0 %copy.9 = bf16[1,2,200,8,128]{4,3,2,1,0:T(8,128)(2,1)} copy(bf16[1,2,200,8,128]{4,2,3,1,0:T(8,128)(2,1)S(1)} %slice_bitcast_fusion) | data formatting | bytes 1638400 | tf_op jit(solution)/shard_map/broadcast_in_dim | solution.py:372
  (2 shorter events, 0.1 us)
Async XLA Ops:
  0.0 1.1 %copy-start = (bf16[2,200,8,128]{3,2,1,0:T(8,128)(2,1)S(1)}, bf16[2,200,8,128]{3,2,1,0:T(8,128)(2,1)}, u32[]{:S(2)}) copy-start(bf16[2,200,8,128]{3,2,1,0:T(8,128)(2,1)} %param.7) | copy-start | bytes 2457604
  1.2 1.0 %copy-start.1 = (bf16[1,200,800]{2,1,0:T(8,128)(2,1)S(1)}, bf16[1,200,800]{2,1,0:T(8,128)(2,1)}, u32[]{:S(2)}) copy-start(bf16[1,200,800]{2,1,0:T(8,128)(2,1)} %param.11) | copy-start | bytes 960004
  1.3 1.1 %copy-start.2 = (bf16[1,800,200]{1,2,0:T(8,128)(2,1)S(1)}, bf16[1,800,200]{1,2,0:T(8,128)(2,1)}, u32[]{:S(2)}) copy-start(bf16[1,800,200]{1,2,0:T(8,128)(2,1)} %param.13) | copy-start | bytes 960004
  1.3 1.1 %copy-start.3 = (f32[1,200,49]{1,0,2:T(1,128)S(1)}, f32[1,200,49]{1,0,2:T(1,128)}, u32[]{:S(2)}) copy-start(f32[1,200,49]{1,0,2:T(1,128)} %param.9) | copy-start | bytes 117604
  1.3 1.1 %copy-start.4 = (f32[1,800]{1,0:T(1,128)S(1)}, f32[1,800]{1,0:T(1,128)}, u32[]{:S(2)}) copy-start(f32[1,800]{1,0:T(1,128)} %bias_ref.1) | copy-start | bytes 9604
  1.3 1.1 %copy-start.5 = (f32[1,200]{1,0:T(1,128)S(1)}, f32[1,200]{1,0:T(1,128)}, u32[]{:S(2)}) copy-start(f32[1,200]{1,0:T(1,128)} %gain_ref.1) | copy-start | bytes 2404
  1.3 1.0 %copy-start.6 = (s32[1,16]{1,0:T(1,128)S(1)}, s32[1,16]{1,0:T(1,128)}, u32[]{:S(2)}) copy-start(s32[1,16]{1,0:T(1,128)} %tiles_ref.1) | copy-start | bytes 196
